TPU v7x, 32 devices: a whole 2x2x4 slice. The times are simulated.
32 devices in a mesh: grp: 4 (over x, core), pair: 8 (over z, y).
Axes of the slice: x: 2, y: 2, z: 4, core: 2. Of those that a mesh axis runs over, the one named last changes fastest.
Arguments:
- chol: bfloat16 [128, 1024, 1024], P(None, 'pair'), may hold values from -0.1875 to 0.1875
- trial: bfloat16 [1024, 512], replicated, may hold values from -2 to 2
- walkers: float32 [32, 1024, 512], P(('grp', 'pair')), may hold values from -10 to 10
- fields: float32 [32, 128], P('grp'), may hold values from -6 to 6
- weights: float32 [32], P(('grp', 'pair')), may hold values from 0.5 to 5
Outputs:
- new_walkers: float32 [32, 1024, 512], P(('grp', 'pair'))
- half_green: float32 [32, 1024, 512], P(('grp', 'pair'))
- new_weights: float32 [32], P(('grp', 'pair'))
All inputs are finite; a program needn't handle non-finite values.
Results may differ from a plain program's by a relative error of at most 0.012.
The roundings to bfloat16 on the way count: a program that leaves them out, or rounds other values in their place, can miss the bound.
Values may be sent and summed in bfloat16 or wider, within the bound.
A program may use at most 128 MiB of HBM per device.

v0:
```python
import jax
import jax.numpy as jnp
from jax import lax
from jax.sharding import PartitionSpec as P

TAYLOR = 4
NS_ITERS = 3


root_step = 0.07


def newton(inner):
    size = inner.shape[-1]
    entries = jnp.diagonal(inner, axis1=1, axis2=2)
    inverse = jnp.eye(size, dtype=jnp.float32)[None] / entries[:, None, :]
    for sweep in range(NS_ITERS):
        product = jnp.einsum("wij,wjk->wik", inner, inverse, precision=lax.Precision.HIGHEST)
        inverse = 2.0 * inverse - jnp.einsum(
            "wij,wjk->wik", inverse, product, precision=lax.Precision.HIGHEST
        )
    return inverse


def solve_half(trial_wide, orbitals):
    inner = jnp.einsum("mi,wmj->wij", trial_wide, orbitals, precision=lax.Precision.HIGHEST)
    inverse = newton(inner)
    return jnp.einsum("wmi,wij->wmj", orbitals, inverse, precision=lax.Precision.HIGHEST)


def per_device(chol, trial, walkers, fields, weights):
    own_count = walkers.shape[0]
    vectors = chol.shape[0]
    block_rows = chol.shape[1]
    width = chol.shape[2]
    trial_wide = trial.astype(jnp.float32)
    theta = solve_half(trial_wide, walkers).astype(jnp.bfloat16)
    theta_block = lax.all_to_all(theta, "pair", split_axis=1, concat_axis=0, tiled=True)
    green_block = jnp.einsum(
        "wri,qi->wrq", theta_block, trial, preferred_element_type=jnp.float32
    ).astype(jnp.bfloat16)
    group_count = green_block.shape[0]
    chol_flat = chol.reshape(vectors, block_rows * width)
    partial_bias = lax.dot_general(
        green_block.reshape(group_count, block_rows * width),
        chol_flat,
        (((1,), (1,)), ((), ())),
        preferred_element_type=jnp.float32,
    )
    bias = lax.psum(partial_bias, "pair")
    xbar = -root_step * bias
    shifted = (fields - xbar).astype(jnp.bfloat16)
    op_block = (
        (root_step * jnp.dot(shifted, chol_flat, preferred_element_type=jnp.float32))
        .reshape(group_count, block_rows, width)
        .astype(jnp.bfloat16)
    )
    operator = lax.all_to_all(op_block, "pair", split_axis=0, concat_axis=1, tiled=True)
    term = walkers
    total = walkers
    for order in range(1, TAYLOR + 1):
        term = jnp.einsum(
            "wpq,wqi->wpi", operator, term.astype(jnp.bfloat16), preferred_element_type=jnp.float32
        ) / float(order)
        total = total + term
    half_green = solve_half(trial_wide, total)
    start = lax.axis_index("pair") * own_count
    own_draws = lax.dynamic_slice_in_dim(fields, start, own_count, 0)
    own_xbar = lax.dynamic_slice_in_dim(xbar, start, own_count, 0)
    raw = weights * jnp.exp(jnp.sum(own_draws * own_xbar - 0.5 * own_xbar * own_xbar, axis=1))
    whole = lax.psum(jnp.sum(raw), ("grp", "pair"))
    count_all = own_count * lax.axis_size("grp") * lax.axis_size("pair")
    new_weights = raw * (count_all / whole)
    return (total, half_green, new_weights)


def solution(mesh):
    placed = (
        P(None, "pair", None),
        P(),
        P(("grp", "pair"), None, None),
        P("grp", None),
        P(("grp", "pair")),
    )
    return jax.shard_map(
        per_device,
        mesh=mesh,
        in_specs=placed,
        out_specs=(
            P(("grp", "pair"), None, None),
            P(("grp", "pair"), None, None),
            P(("grp", "pair")),
        ),
        check_vma=False,
    )
```

profile of v0, /device:TPU:0, one launch (start us, length us, event | category | flops | bytes accessed | tf_op | source)
XLA Modules:
  0.0 290.8 jit_solution(311278721584642162)
XLA Ops:
  0.6 0.0 copy-start
  0.7 1.2 copy-done
  1.9 3.4 %fusion.9 = f32[512,512]{1,0:T(8,128)S(1)} fusion(bf16[1024,512]{1,0:T(8,128)(2,1)S(1)} %copy-done, f32[1,1024,512]{2,1,0:T(8,128)} %param.7), kind=kOutput, calls=%fused_computation.16 | convolution fusion | flops 3221225472 | bytes 4194304 | tf_op jit(solution)/shard_map/mi,wmj->wij/dot_general | solution.py:26
  5.3 4.7 %gather_fusion = f32[512]{0:T(512)S(1)} fusion(f32[512,512]{0,1:T(8,128)S(1)} %bitcast.100, s32[512]{0:T(512)S(1)} %bitcast.95), kind=kCustom, calls=%fused_computation | custom fusion | bytes 8192 | tf_op jit(solution)/shard_map/jit(diagonal)/gather | solution.py:15
  10.0 1.8 fusion.40
  11.9 1.8 convolution_subtract_fusion.5
  13.7 1.9 fusion.50
  15.6 1.9 convolution_subtract_fusion.4
  17.5 1.9 fusion.51
  19.4 0.0 copy-start.1
  19.4 1.9 convolution_subtract_fusion.3
  21.3 0.0 copy-done.1
  21.3 8.1 %fusion.20 = bf16[1,1024,512]{1,2,0:T(8,128)(2,1)} fusion(f32[512,512]{1,0:T(8,128)S(1)} %convolution_subtract_fusion.3, f32[1,1024,512]{2,1,0:T(8,128)S(1)} %copy-done.1), kind=kOutput, calls=%fused_computation.26 | convolution fusion | flops 3221749760 | bytes 4194304 | tf_op jit(solution)/shard_map/wmi,wij->wmj/dot_general | solution.py:28
  29.4 6.0 %copy.14 = bf16[1,1024,512]{2,0,1:T(2,128)(2,1)} copy(bf16[1,1024,512]{1,2,0:T(8,128)(2,1)} %fusion.20) | data formatting | bytes 2097152 | tf_op jit(solution)/shard_map/convert_element_type | solution.py:37
  35.4 0.5 broadcast.74
  35.9 9.0 %reduce.1 = bf16[1024,512]{1,0:T(8,128)(2,1)} reduce(bf16[1024,1,512]{2,1,0:T(2,128)(2,1)} %bitcast.103, bf16[]{:T(256)} %broadcast.74), dimensions={1}, to_apply=%bitcast.64.reduce_sub_computation | reduce | bytes 2097154
  44.9 2.6 reshape.206
  47.5 7.3 %all-to-all-start = ((bf16[8,2,32768]{2,1,0:T(2,128)(2,1)}), bf16[8,2,32768]{2,1,0:T(2,128)(2,1)}, u32[]{:S(2)}, u32[]{:S(2)}) async-start(bf16[8,2,32768]{2,1,0:T(2,128)(2,1)} %reshape.206), calls=%async_computation | async-start | bytes 2097152 | tf_op jit(solution)/shard_map/all_to_all | solution.py:38
  54.8 30.7 %copy.19 = bf16[16,8,128,1024]{3,1,2,0:T(8,128)(2,1)} copy(bf16[16,8,128,1024]{3,2,1,0:T(8,128)(2,1)} %bitcast.98) | data formatting | bytes 67108864
  85.4 0.0 all-to-all-done
  85.4 5.8 %reshape.207 = bf16[1024,1,512]{2,1,0:T(2,128)(2,1)} reshape(bf16[8,2,32768]{2,1,0:T(2,128)(2,1)} %all-to-all-done) | data formatting | bytes 2097152
  91.2 2.8 copy.18
  94.1 54.4 %fusion.23 = f32[8,128]{1,0:T(8,128)S(1)} fusion(bf16[128,128,1024]{2,1,0:T(8,128)(2,1)} %param.5, bf16[1024,512]{1,0:T(8,128)(2,1)S(1)} %copy-done, bf16[8,128,512]{2,1,0:T(8,128)(2,1)} %bitcast.104), kind=kOutput, calls=%fused_computation.33 | convolution fusion | flops 1343225856 | bytes 35655680 | tf_op jit(solution)/shard_map/dot_general | solution.py:44
  148.5 21.8 %psum.14 = f32[8,128]{1,0:T(8,128)S(1)} all-reduce(f32[8,128]{1,0:T(8,128)S(1)} %fusion.23), channel_id=1, replica_groups=mesh['grp'=4,'pair'=8] {'pair'}, use_global_device_ids=true, to_apply=%region_0.1 | all-reduce | flops 1024 | bytes 8192 | tf_op jit(solution)/shard_map/psum | solution.py:50
  170.3 0.0 copy-done.4
  170.3 12.8 %fusion = bf16[8,131072]{1,0:T(8,128)(2,1)S(1)} fusion(bf16[128,131072]{1,0:T(8,128)(2,1)} %bitcast.97, f32[8,128]{1,0:T(8,128)S(1)} %copy-done.4, f32[8,128]{1,0:T(8,128)S(1)} %psum.14), kind=kOutput, calls=%fused_computation.3 | convolution fusion | flops 270535680 | bytes 35659776 | tf_op jit(solution)/shard_map/dot_general | solution.py:54
  183.2 2.5 copy.17
  185.6 4.3 %all-to-all-start.1 = ((bf16[8,128,1024]{2,1,0:T(8,128)(2,1)}), bf16[8,128,1024]{2,1,0:T(8,128)(2,1)}, u32[]{:S(2)}, u32[]{:S(2)}) async-start(bf16[8,128,1024]{2,1,0:T(8,128)(2,1)} %copy.17), calls=%async_computation.1 | async-start | bytes 4194304 | tf_op jit(solution)/shard_map/all_to_all | solution.py:58
  190.6 0.6 fusion.47
  191.9 62.4 %psum.15 = f32[]{:T(128)} all-reduce(f32[]{:T(128)} %bitcast.22), channel_id=1, replica_groups=mesh['grp'=4,'pair'=8] {'grp','pair'}, use_global_device_ids=true, to_apply=%region_2.3 | all-reduce | flops 1 | bytes 8 | tf_op jit(solution)/shard_map/psum | solution.py:71
  255.0 0.0 all-to-all-done.1
  255.0 2.8 fusion.29
  257.9 2.8 fusion.37
  260.7 2.9 fusion.28
  263.6 3.2 %bitcast_add_fusion = f32[1,1024,512]{2,1,0:T(8,128)S(1)} fusion(f32[1,1024,512]{2,1,0:T(8,128)S(1)} %copy-done.1, f32[1024,512]{1,0:T(8,128)S(1)} %fusion.29, f32[1024,512]{1,0:T(8,128)S(1)} %fusion.28, f32[1024,512]{1,0:T(8,128)S(1)} %fusion.37, bf16[1024,1024]{1,0:T(8,128)(2,1)} %bitcast.10), kind=kOutput, calls=%fused_computation.10 | convolution fusion | flops 1078460416 | bytes 12582912 | tf_op jit(solution)/shard_map/wpq,wqi->wpi/dot_general | solution.py:62
  266.8 0.0 copy-start.2
  266.8 1.9 fusion.5
  268.7 0.0 copy-done.2
  268.7 4.7 %gather_fusion.1 = f32[512]{0:T(512)S(1)} fusion(f32[512,512]{0,1:T(8,128)S(1)} %bitcast.99, s32[512]{0:T(512)S(1)} %bitcast.96), kind=kCustom, calls=%fused_computation.1 | custom fusion | bytes 8192 | tf_op jit(solution)/shard_map/jit(diagonal)/gather | solution.py:15
  273.5 1.8 fusion.41
  275.3 1.8 convolution_subtract_fusion.2
  277.1 1.9 fusion.52
  279.0 1.9 convolution_subtract_fusion.1
  280.9 1.9 fusion.53
  282.8 0.0 copy-start.3
  282.8 1.9 convolution_subtract_fusion
  284.7 0.0 copy-done.3
  284.7 4.8 %fusion.14 = f32[1,1024,512]{2,1,0:T(8,128)} fusion(f32[512,512]{1,0:T(8,128)S(1)} %convolution_subtract_fusion, f32[1,1024,512]{2,1,0:T(8,128)S(1)} %copy-done.3), kind=kOutput, calls=%fused_computation.22 | convolution fusion | flops 3221225472 | bytes 5242880 | tf_op jit(solution)/shard_map/wmi,wij->wmj/dot_general | solution.py:28
  (3 shorter events, 0.0 us)
Async XLA Ops:
  0.6 1.2 copy-start
  19.4 1.9 copy-start.1
  47.5 37.9 %all-to-all-start = ((bf16[8,2,32768]{2,1,0:T(2,128)(2,1)}), bf16[8,2,32768]{2,1,0:T(2,128)(2,1)}, u32[]{:S(2)}, u32[]{:S(2)}) async-start(bf16[8,2,32768]{2,1,0:T(2,128)(2,1)} %reshape.206), calls=%async_computation | async-start | bytes 2097152 | tf_op jit(solution)/shard_map/all_to_all | solution.py:38
  94.1 76.2 %copy-start.4 = (f32[8,128]{1,0:T(8,128)S(1)}, f32[8,128]{1,0:T(8,128)}, u32[]{:S(2)}) copy-start(f32[8,128]{1,0:T(8,128)} %param.8) | copy-start | bytes 12292
  185.6 69.4 %all-to-all-start.1 = ((bf16[8,128,1024]{2,1,0:T(8,128)(2,1)}), bf16[8,128,1024]{2,1,0:T(8,128)(2,1)}, u32[]{:S(2)}, u32[]{:S(2)}) async-start(bf16[8,128,1024]{2,1,0:T(8,128)(2,1)} %copy.17), calls=%async_computation.1 | async-start | bytes 4194304 | tf_op jit(solution)/shard_map/all_to_all | solution.py:58
  266.8 1.9 copy-start.2
  282.8 1.9 copy-start.3
where the time goes:
time: 294 us; the launch traced here: 291 us
  matrix products  120 us (41%)
  blocking collectives  84.2 us (29%)
  local copies, waits for them, and re-layouts  61.5 us (21%)
  starting transfers between devices  11.6 us (4%)
  other arithmetic  9.62 us (3%)
  between operations  4.25 us (1%)
    psum x1, blocking collectives, per_device(): whole = lax.psum(jnp.sum(raw), ('grp', 'pair'))  62.4 us
    dot_general x1, matrix products, per_device(): lax.dot_general(green_block.reshape(group_count, block_rows * width), cho...  54.4 us
    unnamed x15, local copies, waits for them, and re-layouts  43.6 us
    psum x1, blocking collectives, per_device(): bias = lax.psum(partial_bias, 'pair')  21.8 us
    dot_general x2, matrix products, solve_half(): jnp.einsum('wmi,wij->wmj', orbitals, inverse, precision=lax.Precision.HIG...  12.9 us
    dot_general x1, matrix products, per_device(): jnp.dot(shifted, chol_flat, preferred_element_type=jnp.float32)  12.8 us
    dot_general x4, matrix products, per_device(): jnp.einsum('wpq,wqi->wpi', operator, term.astype(jnp.bfloat16), preferred...  11.7 us
    dot_general x6, matrix products, newton(): jnp.einsum('wij,wjk->wik', inner, inverse, precision=lax.Precision.HIGHEST)  11.3 us
  transfers between devices with their start and end apart: 2, of which 0 were waited for; matrix products, arithmetic and copies ran while one was open for 11% of the time, Pallas kernels for 0%

commit v1 on v0

v1 whole, which is shorter than its diff:
```python
import functools

import jax
import jax.numpy as jnp
from jax import lax
from jax.experimental import pallas as pl
from jax.experimental.pallas import tpu as pltpu
from jax.sharding import PartitionSpec as P

TAYLOR = 4
NS_ITERS = 3

root_step = 0.07

NT = (((1,), (1,)), ((), ()))
MESH = pl.DeviceIdType.MESH


def product(left, right):
    return jnp.dot(left, right, precision=lax.Precision.HIGH)


def newton(inner):
    size = inner.shape[-1]
    diagonal = jnp.eye(size, dtype=jnp.bool_)
    entries = jnp.sum(jnp.where(diagonal, inner, 0.0), axis=0)
    inverse = jnp.where(diagonal, 1.0 / entries[None, :], 0.0)
    for sweep in range(NS_ITERS):
        inverse = 2.0 * inverse - product(inverse, product(inner, inverse))
    return inverse


def solve_half(trial_wide, orbitals):
    inner = lax.dot_general(
        trial_wide, orbitals, (((0,), (0,)), ((), ())), precision=lax.Precision.HIGH
    )
    return product(orbitals, newton(inner))


def step_kernel(
    count,
    groups,
    theta_ref,
    chol_ref,
    trial_ref,
    walker_ref,
    fields_ref,
    weight_ref,
    total_ref,
    new_weight_ref,
    chol_v,
    theta_in,
    green,
    spread,
    op_send,
    op_v,
    red,
    part_send,
    part_recv,
    group_send,
    group_recv,
    term_a,
    term_b,
    chol_sem,
    theta_s,
    theta_r,
    part_s,
    part_r,
    group_s,
    group_r,
    op_s,
    op_r,
):
    me = lax.axis_index("pair")
    grp = lax.axis_index("grp")
    vectors, rows, width = chol_v.shape
    span = spread.shape[0] // count
    bits = span.bit_length() - 1
    blocks = rows // span
    offsets = [(count // 2 + s) % count for s in range(count)]
    offsets = [offset for offset in offsets if offset]

    def peer(offset):
        return lax.rem(me + offset, count)

    def group_peer(offset):
        return lax.rem(grp + offset, groups)

    load = pltpu.make_async_copy(chol_ref, chol_v, chol_sem)
    load.start()

    barrier = pltpu.get_barrier_semaphore()
    for offset in offsets:
        pl.semaphore_signal(
            barrier, inc=1, device_id={"pair": peer(offset)}, device_id_type=MESH
        )
    for offset in range(1, groups):
        pl.semaphore_signal(
            barrier, inc=1, device_id={"grp": group_peer(offset)}, device_id_type=MESH
        )
    pl.semaphore_wait(barrier, count - 1 + groups - 1)

    def theta_copy(offset):
        other = peer(offset)
        start = pl.multiple_of(other * rows, rows)
        return pltpu.make_async_remote_copy(
            src_ref=theta_ref.at[pl.ds(start, rows), :],
            dst_ref=theta_in.at[me],
            send_sem=theta_s.at[offset],
            recv_sem=theta_r.at[offset],
            device_id={"pair": other},
            device_id_type=MESH,
        )

    theta_copies = {offset: theta_copy(offset) for offset in offsets}
    for offset in offsets:
        theta_copies[offset].start()

    mine = pl.multiple_of(me * rows, rows)

    def make_green(block):
        return lax.dot_general(
            block, trial_ref[...], NT, preferred_element_type=jnp.float32
        ).astype(jnp.bfloat16)

    green[me] = make_green(theta_ref[pl.ds(mine, rows), :])
    for offset in reversed(offsets):
        theta_copies[offset].wait_recv()
        source = lax.rem(me + count - offset, count)
        green[source] = make_green(theta_in[source])
    load.wait()

    step = min(vectors, 512 // span)
    lines = step * span
    columns = count * span
    line = lax.broadcasted_iota(jnp.int32, (lines, columns), 0)
    column = lax.broadcasted_iota(jnp.int32, (lines, columns), 1)
    same = (line & (span - 1)) == (column & (span - 1))

    def bias_step(i, carry):
        first = pl.multiple_of(i * step, step)
        total = None
        for b in range(blocks):
            held = chol_v[pl.ds(first, step), b * span : (b + 1) * span, :]
            seen = green[:, b * span : (b + 1) * span, :]
            part = lax.dot_general(
                held.reshape(lines, width),
                seen.reshape(columns, width),
                NT,
                preferred_element_type=jnp.float32,
            )
            total = part if total is None else total + part
        kept = jnp.where(same, total, 0.0)
        red[pl.ds(first, step), :] = jnp.sum(kept.reshape(step, span, columns), axis=1)
        return carry

    lax.fori_loop(0, vectors // step, bias_step, 0)

    row = lax.broadcasted_iota(jnp.int32, (count, columns), 0)
    col = lax.broadcasted_iota(jnp.int32, (count, columns), 1)
    owner = (lax.shift_right_logical(col, bits) == row).astype(jnp.float32)
    partial = lax.dot_general(
        owner,
        red[...],
        NT,
        precision=lax.Precision.HIGHEST,
        preferred_element_type=jnp.float32,
    )
    part_send[0:count, :] = partial
    part_send[count : count + 8, :] = weight_ref[...]

    def part_copy(offset):
        return pltpu.make_async_remote_copy(
            src_ref=part_send,
            dst_ref=part_recv.at[me],
            send_sem=part_s.at[offset],
            recv_sem=part_r.at[offset],
            device_id={"pair": peer(offset)},
            device_id_type=MESH,
        )

    part_copies = [part_copy(offset) for offset in offsets]
    for copy in part_copies:
        copy.start()
    part_recv[me] = part_send[...]
    for copy in part_copies:
        copy.wait_recv()
    bias = part_recv[0, 0:count, :]
    for source in range(1, count):
        bias = bias + part_recv[source, 0:count, :]
    xbar = -root_step * bias
    draws = fields_ref[...]
    shifted = (draws - xbar).astype(jnp.bfloat16)

    wide = jnp.broadcast_to(
        shifted.astype(jnp.float32)[:, None, :], (count, span, vectors)
    )
    wide = wide.reshape(columns, vectors).astype(jnp.bfloat16)
    pick_row = lax.broadcasted_iota(jnp.int32, (vectors, lines), 0)
    pick_col = lax.broadcasted_iota(jnp.int32, (vectors, lines), 1)
    pick_col = lax.shift_right_logical(pick_col, bits)
    a_row = lax.broadcasted_iota(jnp.int32, (columns, lines), 0)
    a_col = lax.broadcasted_iota(jnp.int32, (columns, lines), 1)
    a_same = (a_row & (span - 1)) == (a_col & (span - 1))

    def spread_step(i, carry):
        pick = jnp.where(pick_row == pick_col + i * step, 1.0, 0.0).astype(jnp.bfloat16)
        value = jnp.dot(wide, pick, preferred_element_type=jnp.float32)
        start = pl.multiple_of(i * lines, lines)
        spread[:, pl.ds(start, lines)] = jnp.where(a_same, value, 0.0).astype(jnp.bfloat16)
        return carry

    lax.fori_loop(0, vectors // step, spread_step, 0)

    def op_copy(b, offset):
        other = peer(offset)
        start = pl.multiple_of(b * span, span)
        place = pl.multiple_of(me * rows + b * span, span)
        return pltpu.make_async_remote_copy(
            src_ref=op_send.at[other, pl.ds(start, span), :],
            dst_ref=op_v.at[pl.ds(place, span), :],
            send_sem=op_s.at[b, offset],
            recv_sem=op_r.at[b, offset],
            device_id={"pair": other},
            device_id_type=MESH,
        )

    tile = 256

    def op_step(b, carry):
        start = pl.multiple_of(b * span, span)

        def op_tile(t, inner):
            left = pl.multiple_of(t * tile, tile)
            held = chol_v[:, pl.ds(start, span), pl.ds(left, tile)]
            value = root_step * jnp.dot(
                spread[...],
                held.reshape(vectors * span, tile),
                preferred_element_type=jnp.float32,
            )
            op_send[:, pl.ds(start, span), pl.ds(left, tile)] = value.astype(
                jnp.bfloat16
            ).reshape(count, span, tile)
            return inner

        lax.fori_loop(0, width // tile, op_tile, 0)
        for offset in offsets:
            op_copy(b, offset).start()
        return carry

    lax.fori_loop(0, blocks, op_step, 0)

    power = jnp.sum(draws * xbar - 0.5 * xbar * xbar, axis=1, keepdims=True)
    raw = part_recv[:, count : count + 8, :][:, 0, :] * jnp.exp(power)
    group_send[...] = jnp.broadcast_to(jnp.sum(raw, axis=0, keepdims=True), group_send.shape)

    def group_copy(offset):
        return pltpu.make_async_remote_copy(
            src_ref=group_send,
            dst_ref=group_recv.at[grp],
            send_sem=group_s.at[offset],
            recv_sem=group_r.at[offset],
            device_id={"grp": group_peer(offset)},
            device_id_type=MESH,
        )

    group_copies = [group_copy(offset) for offset in range(1, groups)]
    for copy in group_copies:
        copy.start()
    group_recv[grp] = group_send[...]

    term_a[...] = walker_ref[...].astype(jnp.bfloat16)

    def first_order(source):
        start = pl.multiple_of(source * rows, rows)
        place = pl.ds(start, rows)
        value = jnp.dot(op_v[place, :], term_a[...], preferred_element_type=jnp.float32)
        total_ref[place, :] = walker_ref[place, :] + value
        term_b[place, :] = value.astype(jnp.bfloat16)

    op_v[pl.ds(mine, rows), :] = op_send[me]
    first_order(me)
    for offset in reversed(offsets):
        for b in range(blocks):
            op_copy(b, offset).wait_recv()
        first_order(lax.rem(me + count - offset, count))

    held, made = term_b, term_a
    chunk = 256
    for order in range(2, TAYLOR + 1):

        def order_step(i, carry, held=held, made=made, order=order):
            place = pl.ds(pl.multiple_of(i * chunk, chunk), chunk)
            value = jnp.dot(
                op_v[place, :], held[...], preferred_element_type=jnp.float32
            ) / float(order)
            total_ref[place, :] = total_ref[place, :] + value
            if order < TAYLOR:
                made[place, :] = value.astype(jnp.bfloat16)
            return carry

        lax.fori_loop(0, width // chunk, order_step, 0)
        held, made = made, held

    for copy in group_copies:
        copy.wait_recv()
    whole = group_recv[0]
    for source in range(1, groups):
        whole = whole + group_recv[source]
    spot = lax.broadcasted_iota(jnp.int32, raw.shape, 0)
    own = jnp.sum(jnp.where(spot == me, raw, 0.0), axis=0, keepdims=True)
    new_weight_ref[...] = own * (float(count * groups) / whole)

    for offset in offsets:
        theta_copies[offset].wait_send()
    for copy in part_copies + group_copies:
        copy.wait_send()
    for offset in offsets:
        for b in range(blocks):
            op_copy(b, offset).wait_send()


def propagate(theta, chol, trial, walker, fields, weights):
    vectors, rows, width = chol.shape
    occupied = trial.shape[1]
    count = lax.axis_size("pair")
    groups = lax.axis_size("grp")
    span = min(rows, max(16, 256 // count))
    blocks = rows // span
    vmem = pl.BlockSpec(memory_space=pltpu.VMEM)
    dma = pltpu.SemaphoreType.DMA
    return pl.pallas_call(
        functools.partial(step_kernel, count, groups),
        out_shape=(
            jax.ShapeDtypeStruct((width, occupied), jnp.float32),
            jax.ShapeDtypeStruct((8, 128), jnp.float32),
        ),
        in_specs=[vmem, pl.BlockSpec(memory_space=pl.ANY), vmem, vmem, vmem, vmem],
        out_specs=(vmem, vmem),
        scratch_shapes=[
            pltpu.VMEM((vectors, rows, width), jnp.bfloat16),
            pltpu.VMEM((count, rows, occupied), jnp.bfloat16),
            pltpu.VMEM((count, rows, width), jnp.bfloat16),
            pltpu.VMEM((count * span, vectors * span), jnp.bfloat16),
            pltpu.VMEM((count, rows, width), jnp.bfloat16),
            pltpu.VMEM((width, width), jnp.bfloat16),
            pltpu.VMEM((vectors, count * span), jnp.float32),
            pltpu.VMEM((count + 8, vectors), jnp.float32),
            pltpu.VMEM((count, count + 8, vectors), jnp.float32),
            pltpu.VMEM((8, 128), jnp.float32),
            pltpu.VMEM((groups, 8, 128), jnp.float32),
            pltpu.VMEM((width, occupied), jnp.bfloat16),
            pltpu.VMEM((width, occupied), jnp.bfloat16),
            dma,
            dma((count,)),
            dma((count,)),
            dma((count,)),
            dma((count,)),
            dma((groups,)),
            dma((groups,)),
            dma((blocks, count)),
            dma((blocks, count)),
        ],
        compiler_params=pltpu.CompilerParams(
            collective_id=0,
            has_side_effects=True,
            vmem_limit_bytes=60 * 1024 * 1024,
        ),
    )(theta, chol, trial, walker, fields, jnp.broadcast_to(weights[:, None], (8, 128)))


def per_device(chol, trial, walkers, fields, weights):
    trial_wide = trial.astype(jnp.float32)
    walker = walkers[0]
    theta = solve_half(trial_wide, walker).astype(jnp.bfloat16)
    total, spread_weight = propagate(theta, chol, trial, walker, fields, weights)
    half_green = solve_half(trial_wide, total)
    return (total[None], half_green[None], spread_weight[0, 0:1])


def solution(mesh):
    placed = (
        P(None, "pair", None),
        P(),
        P(("grp", "pair"), None, None),
        P("grp", None),
        P(("grp", "pair")),
    )
    return jax.shard_map(
        per_device,
        mesh=mesh,
        in_specs=placed,
        out_specs=(
            P(("grp", "pair"), None, None),
            P(("grp", "pair"), None, None),
            P(("grp", "pair")),
        ),
        check_vma=False,
    )
```

time: 294 us -> 141 us (0.48); the launches traced: 291 us -> 141 us
  Pallas kernels: 0 us -> 111 us
  matrix products: 120 us -> 24.3 us
  blocking collectives: 84.2 us -> 0 us
  local copies, waits for them, and re-layouts: 61.5 us -> 4.12 us
  starting transfers between devices: 11.6 us -> 0 us
  other arithmetic: 9.62 us -> 0.01 us
    pallas_call x0 -> x1, Pallas kernels: none -> 111 us  [propagate(): pl.pallas_call(functools.partial(step_kernel, count, groups), out_shape=(...]
    dot_general x22 -> x16, matrix products: 120 us -> 24.3 us  [the longest x14 18.1 us: product(): return jnp.dot(left, right, precision=lax.Precision.HIGH)]
    psum x2 -> x0, blocking collectives: 84.2 us -> none  [the longest x1 62.4 us: per_device(): whole = lax.psum(jnp.sum(raw), ('grp', 'pair'))]
    unnamed x15 -> x7, local copies, waits for them, and re-layouts: 43.6 us -> 2.34 us
    all_to_all x2 -> x0, starting transfers between devices: 11.6 us -> none  [the longest x1 7.27 us: per_device(): lax.all_to_all(theta, 'pair', split_axis=1, concat_axis=0, tiled=True)]
    gather x2 -> x0, local copies, waits for them, and re-layouts: 9.45 us -> none  [newton(): entries = jnp.diagonal(inner, axis1=1, axis2=2)]
    unnamed x1 -> x0, other arithmetic: 9 us -> none
    convert_element_type x2 -> x0, local copies, waits for them, and re-layouts: 8.43 us -> none  [the longest x1 5.95 us: per_device(): theta = solve_half(trial_wide, walkers).astype(jnp.bfloat16)]
  transfers between devices with their start and end apart: 2 -> 0, of which waited for: 0 -> 0; matrix products, arithmetic and copies ran while one was open for 11% -> 0% of each run, Pallas kernels for 0% -> 0%
where the time goes in v1:
time: 141 us
  Pallas kernels  111 us (79%)
  matrix products  24.3 us (17%)
  local copies, waits for them, and re-layouts  4.12 us (3%)
  between operations  1.41 us (1%)
    pallas_call x1, Pallas kernels, propagate(): pl.pallas_call(functools.partial(step_kernel, count, groups), out_shape=(...  111 us
    dot_general x14, matrix products, product(): return jnp.dot(left, right, precision=lax.Precision.HIGH)  18.1 us
    dot_general x2, matrix products, solve_half(): lax.dot_general(trial_wide, orbitals, (((0,), (0,)), ((), ())), precision...  6.15 us

profile of v1, /device:TPU:0, one launch (start us, length us, event | category | flops | bytes accessed | tf_op | source)
XLA Modules:
  0.0 140.9 jit_solution(3314357779724049573)
XLA Ops:
  1.3 0.6 broadcast_in_dim.40.weight_ref
  1.9 3.2 %select_reduce_fusion = (f32[512]{0:T(512)S(1)}, f32[512,512]{1,0:T(8,128)S(1)}) fusion(bf16[1024,512]{1,0:T(8,128)(2,1)} %trial_ref.1, f32[1,1024,512]{2,1,0:T(8,128)} %param.7), kind=kOutput, calls=%fused_computation.21 | convolution fusion | flops 1611398656 | bytes 4196352 | tf_op jit(solution)/shard_map/dot_general | solution.py:34
  5.1 1.0 fusion.6
  6.1 1.0 fusion.8
  7.1 1.0 fusion.31
  8.1 1.0 convolution_subtract_fusion.3
  9.1 1.0 fusion.32
  10.2 0.0 copy-start
  10.2 1.1 convolution_subtract_fusion.2
  11.3 0.5 copy-done
  11.8 2.8 %fusion.14.theta_ref = bf16[1024,512]{1,0:T(8,128)(2,1)} fusion(f32[512,512]{1,0:T(8,128)S(1)} %convolution_subtract_fusion.2, f32[1,1024,512]{2,1,0:T(8,128)S(1)} %copy-done), kind=kOutput, calls=%fused_computation.14 | convolution fusion | flops 1611137024 | bytes 4194304 | tf_op jit(solution)/shard_map/dot_general | solution.py:20
  14.5 0.0 copy-start.2
  14.5 111.1 %shard_map.76 = (f32[1024,512]{1,0:T(8,128)}, f32[8,128]{1,0:T(8,128)}) custom-call(bf16[1024,512]{1,0:T(8,128)(2,1)} %fusion.14.theta_ref, bf16[128,128,1024]{2,1,0:T(8,128)(2,1)} %chol_ref.1, bf16[1024,512]{1,0:T(8,128)(2,1)} %trial_ref.1, f32[1024,512]{1,0:T(8,128)} %bitcast.45, f32[8,128]{1,0:T(8,128)} %fields_ref.1, f32[8,128]{1,0:T(8,128)} %broadcast_in_dim.40.weight_ref), custom_call_target="tpu_custom_call" | custom-call | tf_op jit(solution)/shard_map/pallas_call | solution.py:332
  125.6 1.2 slice.3
  126.8 0.0 copy-done.2
  126.8 2.9 %fusion.15 = (f32[512]{0:T(512)S(1)}, f32[512,512]{0,1:T(8,128)S(1)}) fusion(f32[1024,512]{1,0:T(8,128)} %get-tuple-element.5, bf16[1024,512]{1,0:T(8,128)(2,1)S(1)} %copy-done.2), kind=kOutput, calls=%fused_computation.20 | convolution fusion | flops 1611398656 | bytes 4196352 | tf_op jit(solution)/shard_map/dot_general | solution.py:34
  129.7 1.0 fusion.2
  130.7 1.0 fusion.11
  131.7 1.0 fusion.33
  132.7 1.0 convolution_subtract_fusion.1
  133.8 1.0 fusion.34
  134.8 0.0 copy-start.1
  134.8 1.1 convolution_subtract_fusion
  135.9 0.5 copy-done.1
  136.4 3.2 %convolution_bitcast_fusion = f32[1,1024,512]{2,1,0:T(8,128)} fusion(f32[1024,512]{1,0:T(8,128)S(1)} %copy-done.1, f32[512,512]{1,0:T(8,128)S(1)} %convolution_subtract_fusion), kind=kOutput, calls=%fused_computation.10 | convolution fusion | flops 1610612736 | bytes 5242880 | tf_op jit(solution)/shard_map/dot_general | solution.py:20
  139.5 1.3 copy.12
  (2 shorter events, 0.0 us)
Async XLA Ops:
  10.2 1.6 %copy-start = (f32[1,1024,512]{2,1,0:T(8,128)S(1)}, f32[1,1024,512]{2,1,0:T(8,128)}, u32[]{:S(2)}) copy-start(f32[1,1024,512]{2,1,0:T(8,128)} %param.7) | copy-start | bytes 6291460
  14.5 112.3 %copy-start.2 = (bf16[1024,512]{1,0:T(8,128)(2,1)S(1)}, bf16[1024,512]{1,0:T(8,128)(2,1)}, u32[]{:S(2)}) copy-start(bf16[1024,512]{1,0:T(8,128)(2,1)} %trial_ref.1) | copy-start | bytes 3145732
  134.8 1.6 %copy-start.1 = (f32[1024,512]{1,0:T(8,128)S(1)}, f32[1024,512]{1,0:T(8,128)}, u32[]{:S(2)}) copy-start(f32[1024,512]{1,0:T(8,128)} %get-tuple-element.5) | copy-start | bytes 6291460

commit v2 on v1

--- a/solution.py
+++ b/solution.py
@@ -13,6 +13,7 @@
 root_step = 0.07
 
 NT = (((1,), (1,)), ((), ()))
+TN = (((0,), (0,)), ((), ()))
 MESH = pl.DeviceIdType.MESH
 
 
@@ -24,31 +25,35 @@
     size = inner.shape[-1]
     diagonal = jnp.eye(size, dtype=jnp.bool_)
     entries = jnp.sum(jnp.where(diagonal, inner, 0.0), axis=0)
-    inverse = jnp.where(diagonal, 1.0 / entries[None, :], 0.0)
-    for sweep in range(NS_ITERS):
+    scale = 1.0 / entries
+    first = scale[:, None] * (inner * scale[None, :])
+    inverse = jnp.where(diagonal, 2.0 * scale[None, :], 0.0) - first
+    for sweep in range(1, NS_ITERS):
         inverse = 2.0 * inverse - product(inverse, product(inner, inverse))
     return inverse
 
 
-def solve_half(trial_wide, orbitals):
-    inner = lax.dot_general(
-        trial_wide, orbitals, (((0,), (0,)), ((), ())), precision=lax.Precision.HIGH
-    )
-    return product(orbitals, newton(inner))
+def halves(value):
+    high = value.astype(jnp.bfloat16)
+    return high, (value - high.astype(jnp.float32)).astype(jnp.bfloat16)
 
 
 def step_kernel(
     count,
     groups,
-    theta_ref,
+    inverse_ref,
     chol_ref,
     trial_ref,
     walker_ref,
     fields_ref,
     weight_ref,
     total_ref,
+    inner_ref,
     new_weight_ref,
     chol_v,
+    inverse_high,
+    inverse_low,
+    theta_out,
     theta_in,
     green,
     spread,
@@ -77,17 +82,28 @@
     span = spread.shape[0] // count
     bits = span.bit_length() - 1
     blocks = rows // span
-    offsets = [(count // 2 + s) % count for s in range(count)]
-    offsets = [offset for offset in offsets if offset]
+    offsets = list(range(count - 1, 0, -1))
 
     def peer(offset):
-        return lax.rem(me + offset, count)
+        other = me
+        weight = 1
+        while weight < count:
+            if offset // weight % 2:
+                other = other + weight * (1 - 2 * lax.rem(lax.div(me, weight), 2))
+            weight = 2 * weight
+        return other
 
     def group_peer(offset):
         return lax.rem(grp + offset, groups)
 
-    load = pltpu.make_async_copy(chol_ref, chol_v, chol_sem)
-    load.start()
+    def load(b):
+        place = pl.ds(pl.multiple_of(b * span, span), span)
+        return pltpu.make_async_copy(
+            chol_ref.at[:, place, :], chol_v.at[:, place, :], chol_sem.at[b]
+        )
+
+    for b in range(blocks):
+        load(b).start()
 
     barrier = pltpu.get_barrier_semaphore()
     for offset in offsets:
@@ -98,37 +114,36 @@
         pl.semaphore_signal(
             barrier, inc=1, device_id={"grp": group_peer(offset)}, device_id_type=MESH
         )
+    inverse_high[...], inverse_low[...] = halves(inverse_ref[...])
     pl.semaphore_wait(barrier, count - 1 + groups - 1)
 
-    def theta_copy(offset):
+    def theta_copy(b, offset):
         other = peer(offset)
-        start = pl.multiple_of(other * rows, rows)
+        place = pl.ds(pl.multiple_of(b * span, span), span)
         return pltpu.make_async_remote_copy(
-            src_ref=theta_ref.at[pl.ds(start, rows), :],
-            dst_ref=theta_in.at[me],
-            send_sem=theta_s.at[offset],
-            recv_sem=theta_r.at[offset],
+            src_ref=theta_out.at[other, place, :],
+            dst_ref=theta_in.at[me, place, :],
+            send_sem=theta_s.at[b, offset],
+            recv_sem=theta_r.at[b, offset],
             device_id={"pair": other},
             device_id_type=MESH,
         )
 
-    theta_copies = {offset: theta_copy(offset) for offset in offsets}
-    for offset in offsets:
-        theta_copies[offset].start()
-
-    mine = pl.multiple_of(me * rows, rows)
-
-    def make_green(block):
-        return lax.dot_general(
-            block, trial_ref[...], NT, preferred_element_type=jnp.float32
-        ).astype(jnp.bfloat16)
-
-    green[me] = make_green(theta_ref[pl.ds(mine, rows), :])
-    for offset in reversed(offsets):
-        theta_copies[offset].wait_recv()
-        source = lax.rem(me + count - offset, count)
-        green[source] = make_green(theta_in[source])
-    load.wait()
+    occupied = theta_out.shape[2]
+
+    def theta_block(b, carry):
+        place = pl.ds(pl.multiple_of(b * span, span), span)
+        high, low = halves(walker_ref[:, place, :].reshape(count * span, occupied))
+        value = jnp.dot(high, inverse_low[...], preferred_element_type=jnp.float32)
+        value = value + jnp.dot(low, inverse_high[...], preferred_element_type=jnp.float32)
+        value = value + jnp.dot(high, inverse_high[...], preferred_element_type=jnp.float32)
+        theta_out[:, place, :] = value.astype(jnp.bfloat16).reshape(count, span, occupied)
+        for offset in offsets:
+            theta_copy(b, offset).start()
+        return carry
+
+    lax.fori_loop(0, blocks, theta_block, 0)
+    theta_in[me] = theta_out[me]
 
     step = min(vectors, 512 // span)
     lines = step * span
@@ -136,25 +151,34 @@
     line = lax.broadcasted_iota(jnp.int32, (lines, columns), 0)
     column = lax.broadcasted_iota(jnp.int32, (lines, columns), 1)
     same = (line & (span - 1)) == (column & (span - 1))
-
-    def bias_step(i, carry):
-        first = pl.multiple_of(i * step, step)
-        total = None
-        for b in range(blocks):
-            held = chol_v[pl.ds(first, step), b * span : (b + 1) * span, :]
-            seen = green[:, b * span : (b + 1) * span, :]
-            part = lax.dot_general(
-                held.reshape(lines, width),
-                seen.reshape(columns, width),
-                NT,
-                preferred_element_type=jnp.float32,
+    red[...] = jnp.zeros_like(red)
+
+    def bias_block(b, carry):
+        for offset in offsets:
+            theta_copy(b, offset).wait_recv()
+        start = pl.multiple_of(b * span, span)
+        green[...] = lax.dot_general(
+            trial_ref[...],
+            theta_in[:, pl.ds(start, span), :].reshape(columns, occupied),
+            NT,
+            preferred_element_type=jnp.float32,
+        ).astype(jnp.bfloat16)
+        load(b).wait()
+
+        def bias_step(i, inner):
+            first = pl.multiple_of(i * step, step)
+            held = chol_v[pl.ds(first, step), pl.ds(start, span), :]
+            part = jnp.dot(
+                held.reshape(lines, width), green[...], preferred_element_type=jnp.float32
             )
-            total = part if total is None else total + part
-        kept = jnp.where(same, total, 0.0)
-        red[pl.ds(first, step), :] = jnp.sum(kept.reshape(step, span, columns), axis=1)
+            kept = jnp.where(same, part, 0.0).reshape(step, span, columns)
+            red[pl.ds(first, step), :] = red[pl.ds(first, step), :] + jnp.sum(kept, axis=1)
+            return inner
+
+        lax.fori_loop(0, vectors // step, bias_step, 0)
         return carry
 
-    lax.fori_loop(0, vectors // step, bias_step, 0)
+    lax.fori_loop(0, blocks, bias_block, 0)
 
     row = lax.broadcasted_iota(jnp.int32, (count, columns), 0)
     col = lax.broadcasted_iota(jnp.int32, (count, columns), 1)
@@ -214,11 +238,10 @@
 
     def op_copy(b, offset):
         other = peer(offset)
-        start = pl.multiple_of(b * span, span)
-        place = pl.multiple_of(me * rows + b * span, span)
+        place = pl.ds(pl.multiple_of(b * span, span), span)
         return pltpu.make_async_remote_copy(
-            src_ref=op_send.at[other, pl.ds(start, span), :],
-            dst_ref=op_v.at[pl.ds(place, span), :],
+            src_ref=op_send.at[other, place, :],
+            dst_ref=op_v.at[me, place, :],
             send_sem=op_s.at[b, offset],
             recv_sem=op_r.at[b, offset],
             device_id={"pair": other},
@@ -269,38 +292,55 @@
         copy.start()
     group_recv[grp] = group_send[...]
 
-    term_a[...] = walker_ref[...].astype(jnp.bfloat16)
-
-    def first_order(source):
-        start = pl.multiple_of(source * rows, rows)
-        place = pl.ds(start, rows)
-        value = jnp.dot(op_v[place, :], term_a[...], preferred_element_type=jnp.float32)
-        total_ref[place, :] = walker_ref[place, :] + value
-        term_b[place, :] = value.astype(jnp.bfloat16)
-
-    op_v[pl.ds(mine, rows), :] = op_send[me]
-    first_order(me)
-    for offset in reversed(offsets):
-        for b in range(blocks):
+    term_a[...] = walker_ref[...].reshape(width, occupied).astype(jnp.bfloat16)
+
+    op_v[me] = op_send[me]
+
+    def first_order(b, carry):
+        for offset in offsets:
             op_copy(b, offset).wait_recv()
-        first_order(lax.rem(me + count - offset, count))
-
-    held, made = term_b, term_a
-    chunk = 256
+        place = pl.ds(pl.multiple_of(b * span, span), span)
+        value = jnp.dot(
+            op_v[:, place, :].reshape(columns, width),
+            term_a[...],
+            preferred_element_type=jnp.float32,
+        ).reshape(count, span, occupied)
+        total_ref[:, place, :] = walker_ref[:, place, :] + value
+        term_b[:, place, :] = value.astype(jnp.bfloat16)
+        return carry
+
+    lax.fori_loop(0, blocks, first_order, 0)
+
+    group_rows = max(1, 256 // rows)
+    chunk = group_rows * rows
+    seen, made = term_b, term_a
+    inner_ref[...] = jnp.zeros_like(inner_ref)
     for order in range(2, TAYLOR + 1):
 
-        def order_step(i, carry, held=held, made=made, order=order):
-            place = pl.ds(pl.multiple_of(i * chunk, chunk), chunk)
+        def order_step(i, carry, seen=seen, made=made, order=order):
+            place = pl.ds(i * group_rows, group_rows)
             value = jnp.dot(
-                op_v[place, :], held[...], preferred_element_type=jnp.float32
+                op_v[place].reshape(chunk, width),
+                seen[...].reshape(width, occupied),
+                preferred_element_type=jnp.float32,
             ) / float(order)
-            total_ref[place, :] = total_ref[place, :] + value
-            if order < TAYLOR:
-                made[place, :] = value.astype(jnp.bfloat16)
+            total = total_ref[place].reshape(chunk, occupied) + value
+            total_ref[place] = total.reshape(group_rows, rows, occupied)
+            if order == TAYLOR:
+                bra = trial_ref[pl.ds(pl.multiple_of(i * chunk, chunk), chunk), :]
+                high, low = halves(total)
+                added = lax.dot_general(bra, low, TN, preferred_element_type=jnp.float32)
+                added = added + lax.dot_general(bra, high, TN, preferred_element_type=jnp.float32)
+                inner_ref[...] = inner_ref[...] + added
+            else:
+                if made is term_a:
+                    made[pl.ds(pl.multiple_of(i * chunk, chunk), chunk), :] = value.astype(jnp.bfloat16)
+                else:
+                    made[place] = value.astype(jnp.bfloat16).reshape(group_rows, rows, occupied)
             return carry
 
-        lax.fori_loop(0, width // chunk, order_step, 0)
-        held, made = made, held
+        lax.fori_loop(0, count // group_rows, order_step, 0)
+        seen, made = made, seen
 
     for copy in group_copies:
         copy.wait_recv()
@@ -311,16 +351,15 @@
     own = jnp.sum(jnp.where(spot == me, raw, 0.0), axis=0, keepdims=True)
     new_weight_ref[...] = own * (float(count * groups) / whole)
 
-    for offset in offsets:
-        theta_copies[offset].wait_send()
     for copy in part_copies + group_copies:
         copy.wait_send()
     for offset in offsets:
         for b in range(blocks):
+            theta_copy(b, offset).wait_send()
             op_copy(b, offset).wait_send()
 
 
-def propagate(theta, chol, trial, walker, fields, weights):
+def propagate(inverse, chol, trial, walker, fields, weights):
     vectors, rows, width = chol.shape
     occupied = trial.shape[1]
     count = lax.axis_size("pair")
@@ -332,28 +371,32 @@
     return pl.pallas_call(
         functools.partial(step_kernel, count, groups),
         out_shape=(
-            jax.ShapeDtypeStruct((width, occupied), jnp.float32),
+            jax.ShapeDtypeStruct((count, rows, occupied), jnp.float32),
+            jax.ShapeDtypeStruct((occupied, occupied), jnp.float32),
             jax.ShapeDtypeStruct((8, 128), jnp.float32),
         ),
         in_specs=[vmem, pl.BlockSpec(memory_space=pl.ANY), vmem, vmem, vmem, vmem],
-        out_specs=(vmem, vmem),
+        out_specs=(vmem, vmem, vmem),
         scratch_shapes=[
             pltpu.VMEM((vectors, rows, width), jnp.bfloat16),
+            pltpu.VMEM((occupied, occupied), jnp.bfloat16),
+            pltpu.VMEM((occupied, occupied), jnp.bfloat16),
             pltpu.VMEM((count, rows, occupied), jnp.bfloat16),
-            pltpu.VMEM((count, rows, width), jnp.bfloat16),
+            pltpu.VMEM((count, rows, occupied), jnp.bfloat16),
+            pltpu.VMEM((width, count * span), jnp.bfloat16),
             pltpu.VMEM((count * span, vectors * span), jnp.bfloat16),
             pltpu.VMEM((count, rows, width), jnp.bfloat16),
-            pltpu.VMEM((width, width), jnp.bfloat16),
+            pltpu.VMEM((count, rows, width), jnp.bfloat16),
             pltpu.VMEM((vectors, count * span), jnp.float32),
             pltpu.VMEM((count + 8, vectors), jnp.float32),
             pltpu.VMEM((count, count + 8, vectors), jnp.float32),
             pltpu.VMEM((8, 128), jnp.float32),
             pltpu.VMEM((groups, 8, 128), jnp.float32),
             pltpu.VMEM((width, occupied), jnp.bfloat16),
-            pltpu.VMEM((width, occupied), jnp.bfloat16),
-            dma,
-            dma((count,)),
-            dma((count,)),
+            pltpu.VMEM((count, rows, occupied), jnp.bfloat16),
+            dma((blocks,)),
+            dma((blocks, count)),
+            dma((blocks, count)),
             dma((count,)),
             dma((count,)),
             dma((groups,)),
@@ -366,15 +409,18 @@
             has_side_effects=True,
             vmem_limit_bytes=60 * 1024 * 1024,
         ),
-    )(theta, chol, trial, walker, fields, jnp.broadcast_to(weights[:, None], (8, 128)))
+    )(inverse, chol, trial, walker.reshape(count, rows, occupied), fields, jnp.broadcast_to(weights[:, None], (8, 128)))
 
 
 def per_device(chol, trial, walkers, fields, weights):
-    trial_wide = trial.astype(jnp.float32)
     walker = walkers[0]
-    theta = solve_half(trial_wide, walker).astype(jnp.bfloat16)
-    total, spread_weight = propagate(theta, chol, trial, walker, fields, weights)
-    half_green = solve_half(trial_wide, total)
+    inner = lax.dot_general(
+        trial.astype(jnp.float32), walker, TN, precision=lax.Precision.HIGH
+    )
+    inverse = newton(inner)
+    total, inner_next, spread_weight = propagate(inverse, chol, trial, walker, fields, weights)
+    total = total.reshape(walker.shape)
+    half_green = product(total, newton(inner_next))
     return (total[None], half_green[None], spread_weight[0, 0:1])
 
 

time: 141 us -> 128 us (0.908)
  Pallas kernels: 111 us -> 103 us
  matrix products: 24.3 us -> 17.8 us
    pallas_call x1, Pallas kernels: 111 us -> 103 us  [propagate(): pl.pallas_call(functools.partial(step_kernel, count, groups), out_shape=(...]
    dot_general x14 -> x9, matrix products: 18.1 us -> 14.5 us  [product(): return jnp.dot(left, right, precision=lax.Precision.HIGH)]
    dot_general x2 -> x1, matrix products: 6.15 us -> 3.24 us  [per_device(): lax.dot_general(trial.astype(jnp.float32), walker, TN, precision=lax.Prec...]
where the time goes in v2:
time: 128 us
  Pallas kernels  103 us (80%)
  matrix products  17.8 us (14%)
  local copies, waits for them, and re-layouts  3.66 us (3%)
  other arithmetic  1.38 us (1%)
  between operations  1.36 us (1%)
    pallas_call x1, Pallas kernels, propagate(): pl.pallas_call(functools.partial(step_kernel, count, groups), out_shape=(...  103 us
    dot_general x9, matrix products, product(): return jnp.dot(left, right, precision=lax.Precision.HIGH)  14.5 us
    dot_general x1, matrix products, per_device(): lax.dot_general(trial.astype(jnp.float32), walker, TN, precision=lax.Prec...  3.24 us

profile of v2, /device:TPU:0, one launch (start us, length us, event | category | flops | bytes accessed | tf_op | source)
XLA Modules:
  0.0 127.7 jit_solution(12097803104660447598)
XLA Ops:
  1.3 0.6 broadcast_in_dim.41.weight_ref
  1.9 3.2 %select_reduce_fusion.1 = (f32[512]{0:T(512)S(1)}, f32[512,512]{1,0:T(8,128)S(1)}) fusion(bf16[1024,512]{1,0:T(8,128)(2,1)} %trial_ref.1, f32[1,1024,512]{2,1,0:T(8,128)} %param.7), kind=kOutput, calls=%fused_computation.12 | convolution fusion | flops 1611398656 | bytes 4196352 | tf_op jit(solution)/shard_map/dot_general | solution.py:417
  5.1 1.2 fusion.3
  6.3 1.2 convolution_subtract_fusion.3
  7.5 1.0 fusion.24
  8.5 2.0 %convolution_subtract_fusion.2.inverse_ref = f32[512,512]{1,0:T(8,128)} fusion(f32[512,512]{1,0:T(8,128)S(1)} %convolution_subtract_fusion.3, f32[512,512]{1,0:T(8,128)S(1)} %fusion.24), kind=kOutput, calls=%fused_computation.5 | convolution fusion | flops 805830656 | bytes 3145728 | tf_op jit(solution)/shard_map/dot_general | solution.py:21
  10.5 103.5 %shard_map.76 = (f32[8,128,512]{2,1,0:T(8,128)}, f32[512,512]{1,0:T(8,128)}, f32[8,128]{1,0:T(8,128)}) custom-call(f32[512,512]{1,0:T(8,128)} %convolution_subtract_fusion.2.inverse_ref, bf16[128,128,1024]{2,1,0:T(8,128)(2,1)} %chol_ref.1, bf16[1024,512]{1,0:T(8,128)(2,1)} %trial_ref.1, f32[8,128,512]{2,1,0:T(8,128)} %bitcast.28, f32[8,128]{1,0:T(8,128)} %fields_ref.1, ...), custom_call_target="tpu_custom_call" | custom-call | tf_op jit(solution)/shard_map/pallas_call | solution.py:371
  114.0 1.2 slice.3
  115.2 0.0 copy-start
  115.2 1.4 %select_reduce_fusion = f32[512]{0:T(512)S(1)} fusion(f32[512,512]{1,0:T(8,128)} %get-tuple-element.7), kind=kLoop, calls=%fused_computation.9 | loop fusion | flops 785920 | bytes 1050624 | tf_op jit(solution)/shard_map/reduce_sum | solution.py:27
  116.6 2.8 %fusion.2 = f32[512,512]{1,0:T(8,128)S(1)} fusion(f32[512,512]{1,0:T(8,128)} %get-tuple-element.7, f32[512]{0:T(512)S(1)} %get-tuple-element.10, f32[512]{0:T(512)S(1)} %get-tuple-element.9), kind=kOutput, calls=%fused_computation.8 | convolution fusion | flops 806617088 | bytes 2101248 | tf_op jit(solution)/shard_map/dot_general | solution.py:21
  119.4 0.0 copy-done
  119.4 1.2 convolution_subtract_fusion.1
  120.5 1.0 fusion.25
  121.6 0.0 copy-start.1
  121.6 1.0 convolution_subtract_fusion
  122.6 0.6 copy-done.1
  123.2 3.2 %convolution_bitcast_fusion = f32[1,1024,512]{2,1,0:T(8,128)} fusion(f32[1024,512]{1,0:T(8,128)S(1)} %bitcast.29, f32[512,512]{1,0:T(8,128)S(1)} %convolution_subtract_fusion), kind=kOutput, calls=%fused_computation.2 | convolution fusion | flops 1610612736 | bytes 5242880 | tf_op jit(solution)/shard_map/dot_general | solution.py:21
  126.3 1.3 %copy.10 = f32[1,1024,512]{2,1,0:T(8,128)} copy(f32[1,1024,512]{2,1,0:T(8,128)S(1)} %bitcast.30) | data formatting | bytes 4194304
  (2 shorter events, 0.0 us)
Async XLA Ops:
  115.2 4.2 %copy-start = (f32[512,512]{1,0:T(8,128)S(1)}, f32[512,512]{1,0:T(8,128)}, u32[]{:S(2)}) copy-start(f32[512,512]{1,0:T(8,128)} %get-tuple-element.7) | copy-start | bytes 3145732
  121.6 1.6 %copy-start.1 = (f32[8,128,512]{2,1,0:T(8,128)S(1)}, f32[8,128,512]{2,1,0:T(8,128)}, u32[]{:S(2)}) copy-start(f32[8,128,512]{2,1,0:T(8,128)} %get-tuple-element.6) | copy-start | bytes 6291460
